TPU v7x, 256 devices: a whole 4x4x8 slice. The times are simulated.
256 devices in a mesh: pos: 8 (over y, x_lo), head: 8 (over z), rep: 4 (over x_hi, core).
Axes of the slice: x: 4 (x_hi: 2, x_lo: 2; x = x_hi * 2 + x_lo), y: 4, z: 8, core: 2. Of those that a mesh axis runs over, the one named last changes fastest.
Arguments:
- queries: bfloat16 [2048, 64, 128], P(('pos', 'rep'), 'head'), may hold values from -5 to 5
- doc_keys: bfloat16 [32768, 8, 128], P('pos', 'head'), may hold values from -4.5 to 4.5
- doc_values: bfloat16 [32768, 8, 128], P('pos', 'head'), may hold values from -6 to 6
- suffix_keys: bfloat16 [2048, 128, 8, 128], P(('pos', 'rep'), None, 'head'), may hold values from -10 to 10
- suffix_values: bfloat16 [2048, 128, 8, 128], P(('pos', 'rep'), None, 'head'), may hold values from -6 to 6
- suffix_len: int32 [2048], P(('pos', 'rep')), may hold values from 1 to 128, as said below
- out_weight: bfloat16 [8192, 8192], P('head', ('pos', 'rep')), may hold values from -0.25 to 0.25
Outputs:
- projected: bfloat16 [2048, 8192], P(None, ('pos', 'rep'))
Inputs may be any that keep to these rules, and one draw needn't show every extreme that they name: `suffix_len`: the last live private position holds the new token's key and value.
All inputs are finite; a program needn't handle non-finite values.
Results may differ from a plain program's by a relative error of at most 0.02.
Values may be sent and summed in bfloat16 or wider, within the bound.
No kernel may reach another device: no remote copies, remote signals or barrier semaphores. Data moves between devices by JAX's collectives and lax.ppermute only.
A program may use at most 192 MiB of HBM per device.

v0:
```python
import jax
import jax.numpy as jnp
from jax import lax
from jax.sharding import PartitionSpec as P


def from_behind(value, axis, steps):
    count = lax.axis_size(axis)
    pairs = [(source, (source + steps) % count) for source in range(count)]
    return lax.ppermute(value, axis, pairs)


def absorb(state, query_row_set, keys, values, score_scale):
    top, total, acc = state
    scores = (
        jnp.einsum("rkgd,skd->krgs", query_row_set, keys, preferred_element_type=jnp.float32)
        * score_scale
    )
    top_new = jnp.maximum(top, scores.max(-1))
    fade = jnp.exp(top - top_new)
    terms = jnp.exp(scores - top_new[..., None])
    total = total * fade + terms.sum(-1)
    weights = terms.astype(jnp.bfloat16)
    acc = acc * fade[..., None] + jnp.einsum(
        "krgs,skd->krgd", weights, values, preferred_element_type=jnp.float32
    )
    return (top_new, total, acc)


def suffix_state(query_row_set, suffix_keys, suffix_values, suffix_len, score_scale):
    scores = (
        jnp.einsum(
            "rkgd,rjkd->krgj", query_row_set, suffix_keys, preferred_element_type=jnp.float32
        )
        * score_scale
    )
    active_mask = (
        jnp.arange(suffix_keys.shape[1], dtype=jnp.int32)[None, :] < suffix_len[:, None]
    )[None, :, None, :]
    masked = jnp.where(active_mask, scores, -1e30)
    top = masked.max(-1)
    terms = jnp.where(active_mask, jnp.exp(masked - top[..., None]), 0.0)
    total = terms.sum(-1)
    acc = jnp.einsum(
        "krgj,rjkd->krgd",
        terms.astype(jnp.bfloat16),
        suffix_values,
        preferred_element_type=jnp.float32,
    )
    return (top, total, acc)


def body(queries, doc_keys, doc_values, suffix_keys, suffix_values, suffix_len, out_weight):
    rows = queries.shape[0]
    local_heads = queries.shape[1]
    head_size = queries.shape[2]
    kv_local = doc_keys.shape[1]
    group = local_heads // kv_local
    score_scale = head_size ** (-0.5)
    query_row_set = queries.reshape(rows, kv_local, group, head_size)
    private = suffix_state(query_row_set, suffix_keys, suffix_values, suffix_len, score_scale)

    def turn(step, carry):
        state, keys, values = carry
        state = absorb(state, query_row_set, keys, values, score_scale)
        keys, values = from_behind((keys, values), "pos", 1)
        return (state, keys, values)

    state, keys, values = lax.fori_loop(
        0, lax.axis_size("pos") - 1, turn, (private, doc_keys, doc_values)
    )
    state = absorb(state, query_row_set, keys, values, score_scale)
    top, total, acc = state
    attended = (
        (acc / total[..., None])
        .transpose(1, 0, 2, 3)
        .reshape(rows, local_heads * head_size)
        .astype(jnp.bfloat16)
    )
    terms = jnp.dot(
        lax.all_gather(attended, ("pos", "rep"), axis=0, tiled=True),
        out_weight,
        preferred_element_type=jnp.float32,
    )
    return lax.psum(terms.astype(jnp.bfloat16), "head")


def solution(mesh):
    in_specs = (
        P(("pos", "rep"), "head", None),
        P("pos", "head", None),
        P("pos", "head", None),
        P(("pos", "rep"), None, "head", None),
        P(("pos", "rep"), None, "head", None),
        P(("pos", "rep")),
        P("head", ("pos", "rep")),
    )
    out_specs = P(None, ("pos", "rep"))
    return jax.shard_map(body, mesh=mesh, in_specs=in_specs, out_specs=out_specs, check_vma=False)
```

profile of v0, /device:TPU:2, one launch (start us, length us, event | category | flops | bytes accessed | tf_op | source)
XLA Modules:
  0.0 522.5 jit_solution(8979650046918676955)
XLA Ops:
  16.8 327.2 %while.18 = (s32[]{:T(128)}, f32[1,64,8]{2,1,0:T(8,128)S(1)}, f32[1,64,8]{2,1,0:T(8,128)S(1)}, f32[1,64,8,128]{3,2,1,0:T(8,128)S(1)}, bf16[4096,1,128]{2,0,1:T(8...) while((s32[]{:T(128)}, f32[1,64,8]{2,1,0:T(8,128)S(1)}, ...), condition=%wide.region_5.6_spmd, body=%wide.region_2.5_spmd.sunk | while | flops 1090651648 | bytes 74088640 | solution.py:69
  30.3 5.1 fusion.64
  35.4 9.0 %collective-permute-done = bf16[4096,1,128]{2,0,1:T(8,128)(2,1)} collective-permute-done((bf16[4096,1,128]{2,0,1:T(8,128)(2,1)S(1)}, bf16[4096,1,128]{2,0,1:T(8,128)(2,1)}, u32[]{:S(2)}, u32[]{:S(2)}) %collective-permute-start) | collective-permute-done | bytes 1048608 | tf_op jit(solution)/shard_map/while/body/eval_jaxpr/ppermute | solution.py:10
  44.4 21.0 %collective-permute-done.1 = bf16[4096,1,128]{2,0,1:T(8,128)(2,1)} collective-permute-done((bf16[4096,1,128]{2,0,1:T(8,128)(2,1)}, bf16[4096,1,128]{2,0,1:T(8,128)(2,1)}, u32[]{:S(2)}, u32[]{:S(2)}) %collective-permute-start.1) | collective-permute-done | bytes 1048608 | tf_op jit(solution)/shard_map/while/body/eval_jaxpr/ppermute | solution.py:10
  79.0 5.1 fusion.64
  84.1 9.5 %collective-permute-done = bf16[4096,1,128]{2,0,1:T(8,128)(2,1)} collective-permute-done((bf16[4096,1,128]{2,0,1:T(8,128)(2,1)S(1)}, bf16[4096,1,128]{2,0,1:T(8,128)(2,1)}, u32[]{:S(2)}, u32[]{:S(2)}) %collective-permute-start) | collective-permute-done | bytes 1048608 | tf_op jit(solution)/shard_map/while/body/eval_jaxpr/ppermute | solution.py:10
  93.6 19.7 %collective-permute-done.1 = bf16[4096,1,128]{2,0,1:T(8,128)(2,1)} collective-permute-done((bf16[4096,1,128]{2,0,1:T(8,128)(2,1)}, bf16[4096,1,128]{2,0,1:T(8,128)(2,1)}, u32[]{:S(2)}, u32[]{:S(2)}) %collective-permute-start.1) | collective-permute-done | bytes 1048608 | tf_op jit(solution)/shard_map/while/body/eval_jaxpr/ppermute | solution.py:10
  127.1 5.1 fusion.64
  132.3 9.6 %collective-permute-done = bf16[4096,1,128]{2,0,1:T(8,128)(2,1)} collective-permute-done((bf16[4096,1,128]{2,0,1:T(8,128)(2,1)S(1)}, bf16[4096,1,128]{2,0,1:T(8,128)(2,1)}, u32[]{:S(2)}, u32[]{:S(2)}) %collective-permute-start) | collective-permute-done | bytes 1048608 | tf_op jit(solution)/shard_map/while/body/eval_jaxpr/ppermute | solution.py:10
  141.9 19.2 %collective-permute-done.1 = bf16[4096,1,128]{2,0,1:T(8,128)(2,1)} collective-permute-done((bf16[4096,1,128]{2,0,1:T(8,128)(2,1)}, bf16[4096,1,128]{2,0,1:T(8,128)(2,1)}, u32[]{:S(2)}, u32[]{:S(2)}) %collective-permute-start.1) | collective-permute-done | bytes 1048608 | tf_op jit(solution)/shard_map/while/body/eval_jaxpr/ppermute | solution.py:10
  175.0 5.1 fusion.64
  180.1 9.2 %collective-permute-done = bf16[4096,1,128]{2,0,1:T(8,128)(2,1)} collective-permute-done((bf16[4096,1,128]{2,0,1:T(8,128)(2,1)S(1)}, bf16[4096,1,128]{2,0,1:T(8,128)(2,1)}, u32[]{:S(2)}, u32[]{:S(2)}) %collective-permute-start) | collective-permute-done | bytes 1048608 | tf_op jit(solution)/shard_map/while/body/eval_jaxpr/ppermute | solution.py:10
  189.3 18.7 %collective-permute-done.1 = bf16[4096,1,128]{2,0,1:T(8,128)(2,1)} collective-permute-done((bf16[4096,1,128]{2,0,1:T(8,128)(2,1)}, bf16[4096,1,128]{2,0,1:T(8,128)(2,1)}, u32[]{:S(2)}, u32[]{:S(2)}) %collective-permute-start.1) | collective-permute-done | bytes 1048608 | tf_op jit(solution)/shard_map/while/body/eval_jaxpr/ppermute | solution.py:10
  221.8 5.1 fusion.64
  227.0 9.2 %collective-permute-done = bf16[4096,1,128]{2,0,1:T(8,128)(2,1)} collective-permute-done((bf16[4096,1,128]{2,0,1:T(8,128)(2,1)S(1)}, bf16[4096,1,128]{2,0,1:T(8,128)(2,1)}, u32[]{:S(2)}, u32[]{:S(2)}) %collective-permute-start) | collective-permute-done | bytes 1048608 | tf_op jit(solution)/shard_map/while/body/eval_jaxpr/ppermute | solution.py:10
  236.2 17.7 %collective-permute-done.1 = bf16[4096,1,128]{2,0,1:T(8,128)(2,1)} collective-permute-done((bf16[4096,1,128]{2,0,1:T(8,128)(2,1)}, bf16[4096,1,128]{2,0,1:T(8,128)(2,1)}, u32[]{:S(2)}, u32[]{:S(2)}) %collective-permute-start.1) | collective-permute-done | bytes 1048608 | tf_op jit(solution)/shard_map/while/body/eval_jaxpr/ppermute | solution.py:10
  267.8 5.1 fusion.64
  272.9 9.2 %collective-permute-done = bf16[4096,1,128]{2,0,1:T(8,128)(2,1)} collective-permute-done((bf16[4096,1,128]{2,0,1:T(8,128)(2,1)S(1)}, bf16[4096,1,128]{2,0,1:T(8,128)(2,1)}, u32[]{:S(2)}, u32[]{:S(2)}) %collective-permute-start) | collective-permute-done | bytes 1048608 | tf_op jit(solution)/shard_map/while/body/eval_jaxpr/ppermute | solution.py:10
  282.2 17.6 %collective-permute-done.1 = bf16[4096,1,128]{2,0,1:T(8,128)(2,1)} collective-permute-done((bf16[4096,1,128]{2,0,1:T(8,128)(2,1)}, bf16[4096,1,128]{2,0,1:T(8,128)(2,1)}, u32[]{:S(2)}, u32[]{:S(2)}) %collective-permute-start.1) | collective-permute-done | bytes 1048608 | tf_op jit(solution)/shard_map/while/body/eval_jaxpr/ppermute | solution.py:10
  318.7 9.2 %collective-permute-done = bf16[4096,1,128]{2,0,1:T(8,128)(2,1)} collective-permute-done((bf16[4096,1,128]{2,0,1:T(8,128)(2,1)S(1)}, bf16[4096,1,128]{2,0,1:T(8,128)(2,1)}, u32[]{:S(2)}, u32[]{:S(2)}) %collective-permute-start) | collective-permute-done | bytes 1048608 | tf_op jit(solution)/shard_map/while/body/eval_jaxpr/ppermute | solution.py:10
  328.0 16.0 %collective-permute-done.1 = bf16[4096,1,128]{2,0,1:T(8,128)(2,1)} collective-permute-done((bf16[4096,1,128]{2,0,1:T(8,128)(2,1)}, bf16[4096,1,128]{2,0,1:T(8,128)(2,1)}, u32[]{:S(2)}, u32[]{:S(2)}) %collective-permute-start.1) | collective-permute-done | bytes 1048608 | tf_op jit(solution)/shard_map/while/body/eval_jaxpr/ppermute | solution.py:10
  343.9 5.7 %bitcast_reduce_fusion = (f32[64,8]{0,1:T(8,128)S(1)}, f32[4096,64,8]{0,1,2:T(8,128)}) fusion(bf16[64,8,128]{2,1,0:T(8,128)(2,1)} %param.9, bf16[4096,1,128]{2,0,1:T(8,128)(2,1)} %get-tuple-element.48), kind=kOutput, calls=%fused_computation.17 | convolution fusion | flops 541064704 | bytes 9570304 | tf_op jit(solution)/shard_map/rkgd,skd->krgs/dot_general | solution.py:16
  360.9 72.0 %all-gather.2.cloned.1.call-done = bf16[2048,1024]{1,0:T(8,128)(2,1)} async-done(((bf16[64,1024]{1,0:T(8,128)(2,1)}), bf16[2048,1024]{1,0:T(8,128)(2,1)}) %all-gather.2.cloned.1.call-update) | async-done | bytes 4194320 | tf_op jit(solution)/shard_map/all_gather | solution.py:81
  437.4 76.0 %all-reduce.2.cloned.1.call-done = bf16[2048,256]{1,0:T(8,128)(2,1)} async-done(((bf16[2048,256]{1,0:T(8,128)(2,1)}), bf16[2048,256]{1,0:T(8,128)(2,1)}) %all-reduce.2.cloned.1.call-update) | async-done | bytes 1048592 | tf_op jit(solution)/shard_map/psum | solution.py:85
  (104 shorter events, 129.4 us)
Async XLA Ops:
  6.5 5.5 %copy-start = (bf16[64,128,1,128]{3,1,2,0:T(8,128)(2,1)S(1)}, bf16[64,128,1,128]{3,1,2,0:T(8,128)(2,1)}, u32[]{:S(2)}) copy-start(bf16[64,128,1,128]{3,1,2,0:T(8,128)(2,1)} %param.12) | copy-start | bytes 6291460
  6.5 426.4 %all-gather.2.cloned.1.call-start = ((), (), s32[]{:S(2)}) async-start(), calls=%async_computation | async-start | bytes 4325376 | tf_op jit(solution)/shard_map/all_gather | solution.py:81
  18.0 26.4 %collective-permute-start = (bf16[4096,1,128]{2,0,1:T(8,128)(2,1)S(1)}, bf16[4096,1,128]{2,0,1:T(8,128)(2,1)}, u32[]{:S(2)}, u32[]{:S(2)}) collective-permute-start(bf16[4096,1,128]{2,0,1:T(8,128)(2,1)S(1)} %copy.38), channel_id=1, source_target_pairs={{0,32},{32,64},{64,96},{96,128},{128,160},{160,192},{192,224},{224... | collective-permute-start | bytes 3145736 | tf_op jit(solution)/shard_map/while/body/eval_jaxpr/ppermute | solution.py:10
  21.8 43.7 %collective-permute-start.1 = (bf16[4096,1,128]{2,0,1:T(8,128)(2,1)}, bf16[4096,1,128]{2,0,1:T(8,128)(2,1)}, u32[]{:S(2)}, u32[]{:S(2)}) collective-permute-start(bf16[4096,1,128]{2,0,1:T(8,128)(2,1)} %copy.39), channel_id=1, source_target_pairs={{0,32},{32,64},{64,96},{96,128},{128,160},{160,192},{192,224},{224... | collective-permute-start | bytes 3145736 | tf_op jit(solution)/shard_map/while/body/eval_jaxpr/ppermute | solution.py:10
  25.6 3.2 copy-start.1
  66.7 26.9 %collective-permute-start = (bf16[4096,1,128]{2,0,1:T(8,128)(2,1)S(1)}, bf16[4096,1,128]{2,0,1:T(8,128)(2,1)}, u32[]{:S(2)}, u32[]{:S(2)}) collective-permute-start(bf16[4096,1,128]{2,0,1:T(8,128)(2,1)S(1)} %copy.38), channel_id=1, source_target_pairs={{0,32},{32,64},{64,96},{96,128},{128,160},{160,192},{192,224},{224... | collective-permute-start | bytes 3145736 | tf_op jit(solution)/shard_map/while/body/eval_jaxpr/ppermute | solution.py:10
  71.4 41.9 %collective-permute-start.1 = (bf16[4096,1,128]{2,0,1:T(8,128)(2,1)}, bf16[4096,1,128]{2,0,1:T(8,128)(2,1)}, u32[]{:S(2)}, u32[]{:S(2)}) collective-permute-start(bf16[4096,1,128]{2,0,1:T(8,128)(2,1)} %copy.39), channel_id=1, source_target_pairs={{0,32},{32,64},{64,96},{96,128},{128,160},{160,192},{192,224},{224... | collective-permute-start | bytes 3145736 | tf_op jit(solution)/shard_map/while/body/eval_jaxpr/ppermute | solution.py:10
  74.3 3.2 copy-start.1
  114.5 27.4 %collective-permute-start = (bf16[4096,1,128]{2,0,1:T(8,128)(2,1)S(1)}, bf16[4096,1,128]{2,0,1:T(8,128)(2,1)}, u32[]{:S(2)}, u32[]{:S(2)}) collective-permute-start(bf16[4096,1,128]{2,0,1:T(8,128)(2,1)S(1)} %copy.38), channel_id=1, source_target_pairs={{0,32},{32,64},{64,96},{96,128},{128,160},{160,192},{192,224},{224... | collective-permute-start | bytes 3145736 | tf_op jit(solution)/shard_map/while/body/eval_jaxpr/ppermute | solution.py:10
  120.2 40.9 %collective-permute-start.1 = (bf16[4096,1,128]{2,0,1:T(8,128)(2,1)}, bf16[4096,1,128]{2,0,1:T(8,128)(2,1)}, u32[]{:S(2)}, u32[]{:S(2)}) collective-permute-start(bf16[4096,1,128]{2,0,1:T(8,128)(2,1)} %copy.39), channel_id=1, source_target_pairs={{0,32},{32,64},{64,96},{96,128},{128,160},{160,192},{192,224},{224... | collective-permute-start | bytes 3145736 | tf_op jit(solution)/shard_map/while/body/eval_jaxpr/ppermute | solution.py:10
  122.4 3.2 copy-start.1
  162.3 27.0 %collective-permute-start = (bf16[4096,1,128]{2,0,1:T(8,128)(2,1)S(1)}, bf16[4096,1,128]{2,0,1:T(8,128)(2,1)}, u32[]{:S(2)}, u32[]{:S(2)}) collective-permute-start(bf16[4096,1,128]{2,0,1:T(8,128)(2,1)S(1)} %copy.38), channel_id=1, source_target_pairs={{0,32},{32,64},{64,96},{96,128},{128,160},{160,192},{192,224},{224... | collective-permute-start | bytes 3145736 | tf_op jit(solution)/shard_map/while/body/eval_jaxpr/ppermute | solution.py:10
  168.0 40.0 %collective-permute-start.1 = (bf16[4096,1,128]{2,0,1:T(8,128)(2,1)}, bf16[4096,1,128]{2,0,1:T(8,128)(2,1)}, u32[]{:S(2)}, u32[]{:S(2)}) collective-permute-start(bf16[4096,1,128]{2,0,1:T(8,128)(2,1)} %copy.39), channel_id=1, source_target_pairs={{0,32},{32,64},{64,96},{96,128},{128,160},{160,192},{192,224},{224... | collective-permute-start | bytes 3145736 | tf_op jit(solution)/shard_map/while/body/eval_jaxpr/ppermute | solution.py:10
  170.2 3.2 copy-start.1
  209.2 27.0 %collective-permute-start = (bf16[4096,1,128]{2,0,1:T(8,128)(2,1)S(1)}, bf16[4096,1,128]{2,0,1:T(8,128)(2,1)}, u32[]{:S(2)}, u32[]{:S(2)}) collective-permute-start(bf16[4096,1,128]{2,0,1:T(8,128)(2,1)S(1)} %copy.38), channel_id=1, source_target_pairs={{0,32},{32,64},{64,96},{96,128},{128,160},{160,192},{192,224},{224... | collective-permute-start | bytes 3145736 | tf_op jit(solution)/shard_map/while/body/eval_jaxpr/ppermute | solution.py:10
  214.8 39.1 %collective-permute-start.1 = (bf16[4096,1,128]{2,0,1:T(8,128)(2,1)}, bf16[4096,1,128]{2,0,1:T(8,128)(2,1)}, u32[]{:S(2)}, u32[]{:S(2)}) collective-permute-start(bf16[4096,1,128]{2,0,1:T(8,128)(2,1)} %copy.39), channel_id=1, source_target_pairs={{0,32},{32,64},{64,96},{96,128},{128,160},{160,192},{192,224},{224... | collective-permute-start | bytes 3145736 | tf_op jit(solution)/shard_map/while/body/eval_jaxpr/ppermute | solution.py:10
  217.1 3.2 copy-start.1
  255.2 27.0 %collective-permute-start = (bf16[4096,1,128]{2,0,1:T(8,128)(2,1)S(1)}, bf16[4096,1,128]{2,0,1:T(8,128)(2,1)}, u32[]{:S(2)}, u32[]{:S(2)}) collective-permute-start(bf16[4096,1,128]{2,0,1:T(8,128)(2,1)S(1)} %copy.38), channel_id=1, source_target_pairs={{0,32},{32,64},{64,96},{96,128},{128,160},{160,192},{192,224},{224... | collective-permute-start | bytes 3145736 | tf_op jit(solution)/shard_map/while/body/eval_jaxpr/ppermute | solution.py:10
  260.8 38.9 %collective-permute-start.1 = (bf16[4096,1,128]{2,0,1:T(8,128)(2,1)}, bf16[4096,1,128]{2,0,1:T(8,128)(2,1)}, u32[]{:S(2)}, u32[]{:S(2)}) collective-permute-start(bf16[4096,1,128]{2,0,1:T(8,128)(2,1)} %copy.39), channel_id=1, source_target_pairs={{0,32},{32,64},{64,96},{96,128},{128,160},{160,192},{192,224},{224... | collective-permute-start | bytes 3145736 | tf_op jit(solution)/shard_map/while/body/eval_jaxpr/ppermute | solution.py:10
  263.1 3.2 copy-start.1
  301.0 27.0 %collective-permute-start = (bf16[4096,1,128]{2,0,1:T(8,128)(2,1)S(1)}, bf16[4096,1,128]{2,0,1:T(8,128)(2,1)}, u32[]{:S(2)}, u32[]{:S(2)}) collective-permute-start(bf16[4096,1,128]{2,0,1:T(8,128)(2,1)S(1)} %copy.38), channel_id=1, source_target_pairs={{0,32},{32,64},{64,96},{96,128},{128,160},{160,192},{192,224},{224... | collective-permute-start | bytes 3145736 | tf_op jit(solution)/shard_map/while/body/eval_jaxpr/ppermute | solution.py:10
  306.6 37.3 %collective-permute-start.1 = (bf16[4096,1,128]{2,0,1:T(8,128)(2,1)}, bf16[4096,1,128]{2,0,1:T(8,128)(2,1)}, u32[]{:S(2)}, u32[]{:S(2)}) collective-permute-start(bf16[4096,1,128]{2,0,1:T(8,128)(2,1)} %copy.39), channel_id=1, source_target_pairs={{0,32},{32,64},{64,96},{96,128},{128,160},{160,192},{192,224},{224... | collective-permute-start | bytes 3145736 | tf_op jit(solution)/shard_map/while/body/eval_jaxpr/ppermute | solution.py:10
  349.7 83.2 %copy-start.2 = (bf16[1024,256]{1,0:T(8,128)(2,1)S(1)}, bf16[1024,256]{1,0:T(8,128)(2,1)}, u32[]{:S(2)}) copy-start(bf16[1024,256]{1,0:T(8,128)(2,1)} %param.15) | copy-start | bytes 1572868
  360.9 152.5 %all-reduce.2.cloned.1.call-start = ((), (), s32[]{:S(2)}) async-start(), calls=%async_computation.1 | async-start | bytes 2097152 | tf_op jit(solution)/shard_map/psum | solution.py:85
  (1 other events, 3.2 us)
Sparse Core Ops, SparseCore 0:
  361.0 71.9 all-gather.1
  437.5 75.7 all-reduce.1
where the time goes:
time: 523 us; the launch traced here: 522 us
  waiting for transfers between devices  343 us (66%)
  matrix products  71 us (14%)
  local copies, waits for them, and re-layouts  54.8 us (10%)
  starting transfers between devices  23 us (4%)
  other arithmetic  16.9 us (3%)
  between operations  13.4 us (3%)
    ppermute x14, waiting for transfers between devices, from_behind(): return lax.ppermute(value, axis, pairs)  195 us
    psum x1, waiting for transfers between devices, body(): return lax.psum(terms.astype(jnp.bfloat16), 'head')  76 us
    all_gather x1, waiting for transfers between devices, body(): lax.all_gather(attended, ('pos', 'rep'), axis=0, tiled=True)  72 us
    dot_general x8, matrix products, absorb(): jnp.einsum('krgs,skd->krgd', weights, values, preferred_element_type=jnp....  40.8 us
    another operation x14, local copies, waits for them, and re-layouts  24.4 us
    ppermute x14, starting transfers between devices, from_behind(): return lax.ppermute(value, axis, pairs)  23 us
    while x21, local copies, waits for them, and re-layouts  22.4 us
    dot_general x8, matrix products, absorb(): jnp.einsum('rkgd,skd->krgs', query_row_set, keys, preferred_element_type=...  21.3 us
  transfers between devices with their start and end apart: 16, of which 16 were waited for; matrix products, arithmetic and copies ran while one was open for 15% of the time, Pallas kernels for 0%

commit v1 on v0

v1 whole, which is shorter than its diff:
```python
import functools
import math

import jax
import jax.numpy as jnp
from jax import lax
from jax.experimental import pallas as pl
from jax.experimental.pallas import tpu as pltpu
from jax.sharding import PartitionSpec as P

BF = jnp.bfloat16
F32 = jnp.float32
LOG2E = math.log2(math.e)
VMEM = 48 * 2**20
KEY_TILE = 512
MSG_ROWS = 144


def params():
    return pltpu.CompilerParams(vmem_limit_bytes=VMEM)


def whole(shape):
    return pl.BlockSpec(shape, lambda *_: (0,) * len(shape))


def doc_kernel(q_ref, k_ref, v_ref, out_ref, vt_ref):
    n_keys, head_size = k_ref.shape
    tiles = n_keys // KEY_TILE

    @pl.when(pl.program_id(0) == 0)
    def _():
        for j in range(tiles):
            span = pl.ds(j * KEY_TILE, KEY_TILE)
            vt_ref[pl.ds(0, head_size), span] = v_ref[span, :].T
        vt_ref[pl.ds(head_size, 16), :] = jnp.ones((16, n_keys), BF)

    q = q_ref[0]

    def scores(j):
        return lax.dot_general(
            k_ref[pl.ds(j * KEY_TILE, KEY_TILE), :],
            q,
            (((1,), (1,)), ((), ())),
            preferred_element_type=F32,
        )

    def mix(j, s, shift):
        weights = jnp.exp2(s - shift).astype(BF)
        return jnp.dot(
            vt_ref[:, pl.ds(j * KEY_TILE, KEY_TILE)], weights, preferred_element_type=F32
        )

    def emit(acc, shift):
        total = acc[head_size : head_size + 1]
        lse = shift + jnp.log2(total)
        high = lse.astype(BF).astype(F32)
        mid = (lse - high).astype(BF).astype(F32)
        low = lse - high - mid
        out_ref[0, pl.ds(0, head_size), :] = (acc[:head_size] / total).astype(BF)
        row = lax.broadcasted_iota(jnp.int32, (16, q.shape[0]), 0)
        tail = jnp.where(row == 0, high, jnp.where(row == 1, mid, jnp.where(row == 2, low, 0.0)))
        out_ref[0, pl.ds(head_size, 16), :] = tail.astype(BF)

    s = scores(0)
    shift = s.max(0, keepdims=True)
    acc = None
    for j in range(tiles):
        ahead = scores(j + 1) if j + 1 < tiles else None
        part = mix(j, s, shift)
        acc = part if acc is None else acc + part
        s = ahead
    emit(acc, shift)
    worst = jnp.max(jnp.where(acc[head_size : head_size + 1] < 1e30, 0.0, 1.0))

    @pl.when(worst > 0.5)
    def _():
        def largest(j, top):
            return jnp.maximum(top, scores(j).max(0, keepdims=True))

        top = lax.fori_loop(1, tiles, largest, shift)

        def again(j, total):
            s_j = lax.dot_general(
                k_ref[pl.ds(pl.multiple_of(j * KEY_TILE, KEY_TILE), KEY_TILE), :],
                q,
                (((1,), (1,)), ((), ())),
                preferred_element_type=F32,
            )
            weights = jnp.exp2(s_j - top).astype(BF)
            return total + jnp.dot(
                vt_ref[:, pl.ds(pl.multiple_of(j * KEY_TILE, KEY_TILE), KEY_TILE)],
                weights,
                preferred_element_type=F32,
            )

        emit(lax.fori_loop(0, tiles, again, jnp.zeros(acc.shape, F32)), top)


def doc_attention(q_all, keys, values):
    n_src, rows, head_size = q_all.shape
    n_keys = keys.shape[0]
    work = n_src * rows * n_keys
    return pl.pallas_call(
        doc_kernel,
        grid=(n_src,),
        in_specs=[
            pl.BlockSpec((1, rows, head_size), lambda i: (i, 0, 0)),
            whole((n_keys, head_size)),
            whole((n_keys, head_size)),
        ],
        out_specs=pl.BlockSpec((1, MSG_ROWS, rows), lambda i: (i, 0, 0)),
        out_shape=jax.ShapeDtypeStruct((n_src, MSG_ROWS, rows), BF),
        scratch_shapes=[pltpu.VMEM((MSG_ROWS, n_keys), BF)],
        compiler_params=params(),
        cost_estimate=pl.CostEstimate(
            flops=4 * work * head_size, bytes_accessed=2**22, transcendentals=work
        ),
        name="doc_attention",
    )(q_all, keys, values)


def suffix_kernel(scale, step, len_ref, q_ref, k_ref, v_ref, out_ref, lse_ref):
    base = pl.program_id(0) * step
    slots = k_ref.shape[1]
    lane = lax.broadcasted_iota(jnp.int32, (8, slots), 1)
    scored = [
        lax.dot_general(
            q_ref[i], k_ref[i], (((1,), (1,)), ((), ())), preferred_element_type=F32
        )
        for i in range(step)
    ]
    for i in range(step):
        live = lane < len_ref[base + i]
        s = jnp.where(live, scored[i] * scale, -1e30)
        top = s.max(1, keepdims=True)
        terms = jnp.where(live, jnp.exp2(s - top), 0.0)
        total = terms.sum(1, keepdims=True)
        mixed = jnp.dot(terms.astype(BF), v_ref[i], preferred_element_type=F32) / total
        place = pl.ds((i // 8) * 64 + i % 8, 8, stride=8)
        out_ref[place, :] = mixed
        lse_ref[place, :] = jnp.broadcast_to(top + jnp.log2(total), mixed.shape)


def suffix_attention(queries, keys, values, lens):
    n_req, heads, head_size = queries.shape
    slots = keys.shape[1]
    step = 16
    rows = step * heads
    scale = head_size ** (-0.5) * LOG2E
    wide = jax.ShapeDtypeStruct((n_req * heads, head_size), F32)
    return pl.pallas_call(
        functools.partial(suffix_kernel, scale, step),
        grid=(n_req // step,),
        in_specs=[
            pl.BlockSpec(memory_space=pltpu.SMEM),
            pl.BlockSpec((step, heads, head_size), lambda i: (i, 0, 0)),
            pl.BlockSpec((step, slots, head_size), lambda i: (i, 0, 0)),
            pl.BlockSpec((step, slots, head_size), lambda i: (i, 0, 0)),
        ],
        out_specs=[pl.BlockSpec((rows, head_size), lambda i: (i, 0))] * 2,
        out_shape=[wide, wide],
        compiler_params=params(),
        cost_estimate=pl.CostEstimate(
            flops=4 * n_req * heads * slots * head_size, bytes_accessed=2**22, transcendentals=2**16
        ),
        name="suffix_attention",
    )(lens, queries, keys, values)


def combine_kernel(head_size, msg_ref, own_ref, own_lse_ref, out_ref):
    n_src, _, rows = msg_ref.shape
    lses = []
    for i in range(n_src):
        tail = msg_ref[i, pl.ds(head_size, 16), :].astype(F32)
        lses.append(tail[0:1] + tail[1:2] + tail[2:3])
    top = functools.reduce(jnp.maximum, lses)
    total = None
    acc = None
    for i in range(n_src):
        w = jnp.exp2(lses[i] - top)
        part = msg_ref[i, pl.ds(0, head_size), :].astype(F32) * w
        total = w if total is None else total + w
        acc = part if acc is None else acc + part
    doc = (acc / total).T
    doc_lse = jnp.broadcast_to(top + jnp.log2(total), (head_size, rows)).T
    own_lse = own_lse_ref[...]
    peak = jnp.maximum(doc_lse, own_lse)
    w_doc = jnp.exp2(doc_lse - peak)
    w_own = jnp.exp2(own_lse - peak)
    out_ref[...] = ((doc * w_doc + own_ref[...] * w_own) / (w_doc + w_own)).astype(BF)


def combine(msgs, own, own_lse):
    rows, head_size = own.shape
    return pl.pallas_call(
        functools.partial(combine_kernel, head_size),
        out_shape=jax.ShapeDtypeStruct((rows, head_size), BF),
        compiler_params=params(),
        name="combine",
    )(msgs, own, own_lse)


def project_kernel(steps, *refs):
    first, second = refs[0:4], refs[4:8]
    w_ref, w_far_ref, out_ref, far_ref, acc_ref, acc_far_ref = refs[8:]
    h = pl.program_id(0)

    @pl.when(h == 0)
    def _():
        acc_ref[...] = jnp.zeros_like(acc_ref)
        acc_far_ref[...] = jnp.zeros_like(acc_far_ref)

    def add(pieces):
        cols = []
        for j in range(8):
            rows = jnp.concatenate([piece(j).astype(F32) for piece in pieces], 0)
            cols.append(rows.reshape(-1, 128).astype(BF))
        lhs = jnp.concatenate(cols, 1)
        acc_ref[...] += jnp.dot(lhs, w_ref[...], preferred_element_type=F32)
        acc_far_ref[...] += jnp.dot(lhs, w_far_ref[...], preferred_element_type=F32)

    @pl.when(h < steps // 2)
    def _():
        add([lambda j, dx=dx: first[dx][:, h * 8 + j] for dx in range(4)])

    @pl.when(h >= steps // 2)
    def _():
        add(
            [
                lambda j, dx=dx, dy=dy: second[dy][pl.ds(dx, 1), (h - steps // 2) * 8 + j]
                for dx in range(4)
                for dy in range(4)
            ]
        )

    @pl.when(h == steps - 1)
    def _():
        out_ref[...] = acc_ref[...].astype(BF)
        far_ref[...] = acc_far_ref[...].astype(BF)


def project(first, second, w, w_far):
    steps = 8
    depth = w.shape[0] // steps
    cols = w.shape[1]
    rows = 128
    piece = first[0].shape
    return pl.pallas_call(
        functools.partial(project_kernel, steps),
        grid=(steps,),
        in_specs=[whole(piece)] * 8 + [pl.BlockSpec((depth, cols), lambda i: (i, 0))] * 2,
        out_specs=[whole((rows, cols))] * 2,
        out_shape=[jax.ShapeDtypeStruct((rows, cols), BF)] * 2,
        scratch_shapes=[pltpu.VMEM((rows, cols), F32)] * 2,
        compiler_params=params(),
        cost_estimate=pl.CostEstimate(
            flops=4 * rows * w.shape[0] * cols, bytes_accessed=10 * 2**20, transcendentals=0
        ),
        name="project",
    )(*first, *second, w, w_far)


def place_kernel(where_ref, *refs):
    out_ref = refs[-1]
    y, x, core, z = where_ref[0], where_ref[1], where_ref[2], where_ref[3]
    for s in range(8):
        layer = lax.rem(z + 8 - s, 8)
        for c in range(2):
            src = refs[2 * s + c]
            at_core = core if c == 0 else 1 - core
            for dx in range(4):
                sx = lax.rem(x + 4 - dx, 4)
                for dy in range(4):
                    sy = lax.rem(y + 4 - dy, 4)
                    pos = sy * 2 + lax.rem(sx, 2)
                    rep = (sx // 2) * 2 + at_core
                    out_ref[pos, rep, layer] = src[dx * 4 + dy]


def place(where, pieces, cols):
    return pl.pallas_call(
        place_kernel,
        in_specs=[pl.BlockSpec(memory_space=pltpu.SMEM)] + [whole((16, 8, cols))] * len(pieces),
        out_specs=whole((8, 4, 8, 8, cols)),
        out_shape=jax.ShapeDtypeStruct((8, 4, 8, 8, cols), BF),
        compiler_params=params(),
        name="place",
    )(where, *[p.reshape(16, 8, cols) for p in pieces])


def plane_shift(value, dy, dx):
    pairs = []
    for pos in range(8):
        for rep in range(4):
            y, x, core = pos // 2, (rep // 2) * 2 + pos % 2, rep % 2
            ty, tx = (y + dy) % 4, (x + dx) % 4
            pairs.append((pos * 4 + rep, (ty * 2 + tx % 2) * 4 + (tx // 2) * 2 + core))
    return lax.ppermute(value, ("pos", "rep"), pairs)


def head_shift(value, s):
    return lax.ppermute(value, "head", [(i, (i + s) % 8) for i in range(8)])


def other_core(value):
    return lax.ppermute(value, "rep", [(i, i ^ 1) for i in range(4)])


def body(queries, doc_keys, doc_values, suffix_keys, suffix_values, suffix_len, out_weight):
    n_req, heads, head_size = queries.shape
    keys = doc_keys.reshape(-1, head_size)
    values = doc_values.reshape(-1, head_size)
    s_keys = suffix_keys.reshape(n_req, -1, head_size)
    s_values = suffix_values.reshape(n_req, -1, head_size)
    n_pos = lax.axis_size("pos")

    w_near = lax.all_gather(out_weight, "head", axis=0, tiled=True)
    w_far = other_core(w_near)

    scaled = (queries.astype(F32) * (head_size ** (-0.5) * LOG2E)).astype(BF)
    ordered = scaled.reshape(8, 8, heads, head_size).transpose(0, 2, 1, 3)
    ordered = ordered.reshape(n_req * heads, head_size)
    q_all = lax.all_to_all(
        jnp.broadcast_to(ordered[None], (n_pos,) + ordered.shape), "pos", 0, 0, tiled=True
    )
    own, own_lse = suffix_attention(queries, s_keys, s_values, suffix_len)
    msgs = doc_attention(q_all, keys, values)
    msgs = lax.all_to_all(msgs, "pos", 0, 0, tiled=True)
    attended = combine(msgs, own, own_lse)

    rows = lax.all_to_all(attended.reshape(8, 64, head_size), "head", 0, 0, tiled=True)
    rows = rows.reshape(64, 8, head_size)
    half_a, half_b = rows[:32], rows[32:]
    along_y = jnp.stack([half_a] + [plane_shift(half_a, s, 0) for s in (1, 2, 3)])
    along_x = jnp.stack([half_b] + [plane_shift(half_b, 0, s) for s in (1, 2, 3)])
    first = [along_y] + [plane_shift(along_y, 0, s) for s in (1, 2, 3)]
    second = [along_x] + [plane_shift(along_x, s, 0) for s in (1, 2, 3)]
    near, far = project(first, second, w_near, w_far)
    far = other_core(far)

    pieces = [near, far]
    both = jnp.stack([near, far])
    for s in range(1, 8):
        got = head_shift(both, s)
        pieces += [got[0], got[1]]
    pos, rep, z = lax.axis_index("pos"), lax.axis_index("rep"), lax.axis_index("head")
    where = jnp.stack([pos // 2, (rep // 2) * 2 + pos % 2, rep % 2, z]).astype(jnp.int32)
    cols = out_weight.shape[1]
    return place(where, pieces, cols).reshape(-1, cols)


def solution(mesh):
    in_specs = (
        P(("pos", "rep"), "head", None),
        P("pos", "head", None),
        P("pos", "head", None),
        P(("pos", "rep"), None, "head", None),
        P(("pos", "rep"), None, "head", None),
        P(("pos", "rep")),
        P("head", ("pos", "rep")),
    )
    out_specs = P(None, ("pos", "rep"))
    return jax.shard_map(body, mesh=mesh, in_specs=in_specs, out_specs=out_specs, check_vma=False)
```

time: 523 us -> 239 us (0.46)
  waiting for transfers between devices: 343 us -> 101 us
  matrix products: 71 us -> 0 us
  local copies, waits for them, and re-layouts: 54.8 us -> 6.15 us
  blocking collectives: 0 us -> 34 us
  Pallas kernels: 0 us -> 29.8 us
  starting transfers between devices: 23 us -> 51.2 us
  other arithmetic: 16.9 us -> 1.09 us
    ppermute x14 -> x21, waiting for transfers between devices: 195 us -> 35.8 us  [the longest x7 19.4 us: head_shift(): return lax.ppermute(value, 'head', [(i, (i + s) % 8) for i in range(8)])]
    psum x1 -> x0, waiting for transfers between devices: 76 us -> none  [body(): return lax.psum(terms.astype(jnp.bfloat16), 'head')]
    dot_general x19 -> x0, matrix products: 71 us -> none  [the longest x8 40.8 us: absorb(): jnp.einsum('krgs,skd->krgd', weights, values, preferred_element_type=jnp....]
    all_to_all x0 -> x2, blocking collectives: none -> 34 us  [the longest x1 20.8 us: body(): lax.all_to_all(jnp.broadcast_to(ordered[None], (n_pos,) + ordered.shape),...]
    pallas_call x0 -> x5, Pallas kernels: none -> 29.8 us  [the longest x1 17.7 us: doc_attention(): pl.pallas_call(doc_kernel, grid=(n_src,), in_specs=[pl.BlockSpec((1, rows...]
    another operation x14 -> x7, local copies, waits for them, and re-layouts: 24.4 us -> 0.07 us  [place(): p.reshape(16, 8, cols)]
    ppermute x14 -> x21, starting transfers between devices: 23 us -> 46.5 us  [the longest x12 35.5 us: plane_shift(): return lax.ppermute(value, ('pos', 'rep'), pairs)]
    while x23 -> x0, local copies, waits for them, and re-layouts: 22.5 us -> none
  transfers between devices with their start and end apart: 16 -> 23, of which waited for: 16 -> 13; matrix products, arithmetic and copies ran while one was open for 15% -> 1% of each run, Pallas kernels for 0% -> 9%
where the time goes in v1:
time: 239 us; the launch traced here: 237 us
  waiting for transfers between devices  101 us (42%)
  starting transfers between devices  51.2 us (21%)
  blocking collectives  34 us (14%)
  Pallas kernels  29.8 us (12%)
  between operations  13.6 us (6%)
  local copies, waits for them, and re-layouts  6.15 us (3%)
    all_gather x1, waiting for transfers between devices, body(): w_near = lax.all_gather(out_weight, 'head', axis=0, tiled=True)  59.7 us
    ppermute x12, starting transfers between devices, plane_shift(): return lax.ppermute(value, ('pos', 'rep'), pairs)  35.5 us
    all_to_all x1, blocking collectives, body(): lax.all_to_all(jnp.broadcast_to(ordered[None], (n_pos,) + ordered.shape),...  20.8 us
    ppermute x7, waiting for transfers between devices, head_shift(): return lax.ppermute(value, 'head', [(i, (i + s) % 8) for i in range(8)])  19.4 us
    pallas_call x1, Pallas kernels, doc_attention(): pl.pallas_call(doc_kernel, grid=(n_src,), in_specs=[pl.BlockSpec((1, rows...  17.7 us
    ppermute x12, waiting for transfers between devices, plane_shift(): return lax.ppermute(value, ('pos', 'rep'), pairs)  15.1 us
    all_to_all x1, blocking collectives, body(): lax.all_to_all(attended.reshape(8, 64, head_size), 'head', 0, 0, tiled=True)  13.2 us
    ppermute x7, starting transfers between devices, head_shift(): return lax.ppermute(value, 'head', [(i, (i + s) % 8) for i in range(8)])  10.8 us
  transfers between devices with their start and end apart: 23, of which 13 were waited for; matrix products, arithmetic and copies ran while one was open for 1% of the time, Pallas kernels for 9%

profile of v1, /device:TPU:2, one launch (start us, length us, event | category | flops | bytes accessed | tf_op | source)
XLA Modules:
  0.0 237.2 jit_solution(4960798577346229486)
XLA Ops:
  7.3 59.7 %all-gather.2.cloned.1.call-done.refs_8_ = bf16[8192,256]{1,0:T(8,128)(2,1)} async-done(((bf16[1024,256]{1,0:T(8,128)(2,1)}), bf16[8192,256]{1,0:T(8,128)(2,1)}) %all-gather.2.cloned.1.call-update) | async-done | bytes 4194320 | tf_op jit(solution)/shard_map/all_gather | solution.py:318
  68.1 20.8 %all_to_all.15.q_ref = bf16[8,512,128]{2,1,0:T(8,128)(2,1)S(1)} all-to-all(bf16[8,512,128]{2,1,0:T(8,128)(2,1)S(1)} %broadcast_in_dim.8), channel_id=1, replica_groups=mesh['pos'=8,'head'=8,'rep'=4] {'pos'}, dimensions={0} | all-to-all | bytes 2097152 | tf_op jit(solution)/shard_map/all_to_all | solution.py:324
  88.8 17.7 %doc_attention.1 = bf16[8,144,512]{2,1,0:T(8,128)(2,1)S(1)} custom-call(bf16[8,512,128]{2,1,0:T(8,128)(2,1)S(1)} %all_to_all.15.q_ref, bf16[4096,128]{1,0:T(8,128)(2,1)S(1)} %bitcast.63, bf16[4096,128]{1,0:T(8,128)(2,1)S(1)} %bitcast.64), custom_call_target="tpu_custom_call" | custom-call | flops 8589934592 | bytes 4194304 | tf_op jit(solution)/shard_map/doc_attention/pallas_call | solution.py:104
  107.6 4.8 %all-to-all-start.1 = ((bf16[8,144,512]{2,1,0:T(8,128)(2,1)}), bf16[8,144,512]{2,1,0:T(8,128)(2,1)S(1)}, u32[]{:S(2)}, u32[]{:S(2)}) async-start(bf16[8,144,512]{2,1,0:T(8,128)(2,1)} %copy-done.2), calls=%async_computation.1 | async-start | bytes 2359296 | tf_op jit(solution)/shard_map/all_to_all | solution.py:329
  114.0 2.9 %suffix_attention.1 = (f32[512,128]{1,0:T(8,128)S(1)}, f32[512,128]{1,0:T(8,128)S(1)}) custom-call(s32[64]{0:T(128)S(1)} %copy-done.8, bf16[64,8,128]{2,1,0:T(8,128)(2,1)S(1)} %copy-done.3, bf16[64,128,128]{2,1,0:T(8,128)(2,1)S(1)} %bitcast.56, bf16[64,128,128]{2,1,0:T(8,128)(2,1)S(1)} %bitcast.57), custom_call_target="tpu_custom_call" | custom-call | flops 33554432 | bytes 4194304 | tf_op jit(solution)/shard_map/suffix_attention/pallas_call | solution.py:152
  118.3 5.1 %all-to-all-done.1.msg_ref = bf16[8,144,512]{2,1,0:T(8,128)(2,1)S(1)} async-done(((bf16[8,144,512]{2,1,0:T(8,128)(2,1)}), bf16[8,144,512]{2,1,0:T(8,128)(2,1)S(1)}, u32[]{:S(2)}, u32[]{:S(2)}) %all-to-all-start.1) | async-done | bytes 1179680 | tf_op jit(solution)/shard_map/all_to_all | solution.py:329
  125.8 13.2 %all_to_all.16 = bf16[8,64,128]{2,1,0:T(8,128)(2,1)S(1)} all-to-all(bf16[8,64,128]{2,1,0:T(8,128)(2,1)S(1)} %bitcast.58), channel_id=1, replica_groups=mesh['pos'=8,'head'=8,'rep'=4] {'head'}, dimensions={0} | all-to-all | bytes 262144 | tf_op jit(solution)/shard_map/all_to_all | solution.py:332
  139.0 19.1 %collective-permute-start.6 = (bf16[32,8,128]{2,1,0:T(8,128)(2,1)S(1)}, bf16[32,8,128]{2,1,0:T(8,128)(2,1)S(1)}, u32[]{:S(2)}, u32[]{:S(2)}) collective-permute-start(bf16[32,8,128]{2,1,0:T(8,128)(2,1)S(1)} %bitcast.71), channel_id=1, source_target_pairs={{0,32},{1,33},{2,34},{3,35},{32,2},{33,3},{34,0},{35,1},{64,96},{6... | collective-permute-start | bytes 196616 | tf_op jit(solution)/shard_map/ppermute | solution.py:299
  158.4 2.5 %collective-permute-start.8 = (bf16[32,8,128]{2,1,0:T(8,128)(2,1)S(1)}, bf16[32,8,128]{2,1,0:T(8,128)(2,1)S(1)}, u32[]{:S(2)}, u32[]{:S(2)}) collective-permute-start(bf16[32,8,128]{2,1,0:T(8,128)(2,1)S(1)} %bitcast.73), channel_id=1, source_target_pairs={{0,34},{1,35},{2,32},{3,33},{32,0},{33,1},{34,2},{35,3},{64,98},{6... | collective-permute-start | bytes 196616 | tf_op jit(solution)/shard_map/ppermute | solution.py:299
  161.0 2.9 %collective-permute-done.7 = bf16[32,8,128]{2,1,0:T(8,128)(2,1)S(1)} collective-permute-done((bf16[32,8,128]{2,1,0:T(8,128)(2,1)S(1)}, bf16[32,8,128]{2,1,0:T(8,128)(2,1)S(1)}, u32[]{:S(2)}, u32[]{:S(2)}) %collective-permute-start.7) | collective-permute-done | bytes 65568 | tf_op jit(solution)/shard_map/ppermute | solution.py:299
  166.9 2.7 %collective-permute-start.1 = (bf16[32,8,128]{2,1,0:T(8,128)(2,1)S(1)}, bf16[32,8,128]{2,1,0:T(8,128)(2,1)S(1)}, u32[]{:S(2)}, u32[]{:S(2)}) collective-permute-start(bf16[32,8,128]{2,1,0:T(8,128)(2,1)S(1)} %bitcast.68), channel_id=1, source_target_pairs={{0,128},{1,129},{2,130},{3,131},{32,160},{33,161},{34,162},{35,163... | collective-permute-start | bytes 196616 | tf_op jit(solution)/shard_map/ppermute | solution.py:299
  169.5 4.4 %collective-permute-done = bf16[32,8,128]{2,1,0:T(8,128)(2,1)S(1)} collective-permute-done((bf16[32,8,128]{2,1,0:T(8,128)(2,1)S(1)}, bf16[32,8,128]{2,1,0:T(8,128)(2,1)S(1)}, u32[]{:S(2)}, u32[]{:S(2)}) %collective-permute-start) | collective-permute-done | bytes 65568 | tf_op jit(solution)/shard_map/ppermute | solution.py:299
  174.0 2.5 %collective-permute-start.9 = (bf16[4,32,8,128]{3,2,1,0:T(8,128)(2,1)S(1)}, bf16[4,32,8,128]{3,2,1,0:T(8,128)(2,1)S(1)}, u32[]{:S(2)}, u32[]{:S(2)}) collective-permute-start(bf16[4,32,8,128]{3,2,1,0:T(8,128)(2,1)S(1)} %pad_maximum_fusion.1.refs_4_), channel_id=1, source_target_pairs={{0,64},{1,65},{2,66},{3,67},{32,96},{33,97},{34,98},{35,99},{64,12... | collective-permute-start | bytes 786440 | tf_op jit(solution)/shard_map/ppermute | solution.py:299
  179.1 2.9 %collective-permute-start.4 = (bf16[4,32,8,128]{3,2,1,0:T(8,128)(2,1)S(1)}, bf16[4,32,8,128]{3,2,1,0:T(8,128)(2,1)S(1)}, u32[]{:S(2)}, u32[]{:S(2)}) collective-permute-start(bf16[4,32,8,128]{3,2,1,0:T(8,128)(2,1)S(1)} %pad_maximum_fusion.refs_0_), channel_id=1, source_target_pairs={{0,2},{1,3},{2,0},{3,1},{32,34},{33,35},{34,32},{35,33},{64,66},{6... | collective-permute-start | bytes 786440 | tf_op jit(solution)/shard_map/ppermute | solution.py:299
  184.7 2.3 collective-permute-done.4.refs_2_
  187.0 2.7 %collective-permute-done.5.refs_3_ = bf16[4,32,8,128]{3,2,1,0:T(8,128)(2,1)S(1)} collective-permute-done((bf16[4,32,8,128]{3,2,1,0:T(8,128)(2,1)S(1)}, bf16[4,32,8,128]{3,2,1,0:T(8,128)(2,1)S(1)}, u32[]{:S(2)}, u32[]{:S(2)}) %collective-permute-start.5) | collective-permute-done | bytes 262176 | tf_op jit(solution)/shard_map/ppermute | solution.py:299
  189.8 6.7 %project.1 = (bf16[128,256]{1,0:T(8,128)(2,1)S(1)}, bf16[128,256]{1,0:T(8,128)(2,1)S(1)}) custom-call(bf16[4,32,8,128]{3,2,1,0:T(8,128)(2,1)S(1)} %pad_maximum_fusion.refs_0_, bf16[4,32,8,128]{3,2,1,0:T(8,128)(2,1)S(1)} %collective-permute-done.3.refs_1_, bf16[4,32,8,128]{3,2,1,0:T(8,128)(2,1)S(1)} %collective-permute-done.4.refs_2_, ...), custom_call_target="tpu_custom_call" | custom-call | flops 1073741824 | bytes 10485760 | tf_op jit(solution)/shard_map/project/pallas_call | solution.py:249
  199.0 3.9 %collective-permute-start.18 = (bf16[2,128,256]{2,1,0:T(8,128)(2,1)S(1)}, bf16[2,128,256]{2,1,0:T(8,128)(2,1)S(1)}, u32[]{:S(2)}, u32[]{:S(2)}) collective-permute-start(bf16[2,128,256]{2,1,0:T(8,128)(2,1)S(1)} %pad_maximum_fusion.2), channel_id=1, source_target_pairs={{0,20},{4,24},{8,28},{12,0},{16,4},{20,8},{24,12},{28,16},{1,21},{... | collective-permute-start | bytes 393224 | tf_op jit(solution)/shard_map/ppermute | solution.py:303
  202.9 2.0 collective-permute-start.17
  204.9 2.5 %collective-permute-start.16 = (bf16[2,128,256]{2,1,0:T(8,128)(2,1)S(1)}, bf16[2,128,256]{2,1,0:T(8,128)(2,1)S(1)}, u32[]{:S(2)}, u32[]{:S(2)}) collective-permute-start(bf16[2,128,256]{2,1,0:T(8,128)(2,1)S(1)} %pad_maximum_fusion.2), channel_id=1, source_target_pairs={{0,12},{4,16},{8,20},{12,24},{16,28},{20,0},{24,4},{28,8},{1,13},{... | collective-permute-start | bytes 393224 | tf_op jit(solution)/shard_map/ppermute | solution.py:303
  208.8 3.6 %collective-permute-done.19 = bf16[2,128,256]{2,1,0:T(8,128)(2,1)S(1)} collective-permute-done((bf16[2,128,256]{2,1,0:T(8,128)(2,1)S(1)}, bf16[2,128,256]{2,1,0:T(8,128)(2,1)S(1)}, u32[]{:S(2)}, u32[]{:S(2)}) %collective-permute-start.19) | collective-permute-done | bytes 131104 | tf_op jit(solution)/shard_map/ppermute | solution.py:303
  212.5 5.8 %collective-permute-done.18 = bf16[2,128,256]{2,1,0:T(8,128)(2,1)S(1)} collective-permute-done((bf16[2,128,256]{2,1,0:T(8,128)(2,1)S(1)}, bf16[2,128,256]{2,1,0:T(8,128)(2,1)S(1)}, u32[]{:S(2)}, u32[]{:S(2)}) %collective-permute-start.18) | collective-permute-done | bytes 131104 | tf_op jit(solution)/shard_map/ppermute | solution.py:303
  218.3 6.2 %collective-permute-done.16 = bf16[2,128,256]{2,1,0:T(8,128)(2,1)S(1)} collective-permute-done((bf16[2,128,256]{2,1,0:T(8,128)(2,1)S(1)}, bf16[2,128,256]{2,1,0:T(8,128)(2,1)S(1)}, u32[]{:S(2)}, u32[]{:S(2)}) %collective-permute-start.16) | collective-permute-done | bytes 131104 | tf_op jit(solution)/shard_map/ppermute | solution.py:303
  224.6 3.8 %collective-permute-done.14 = bf16[2,128,256]{2,1,0:T(8,128)(2,1)S(1)} collective-permute-done((bf16[2,128,256]{2,1,0:T(8,128)(2,1)S(1)}, bf16[2,128,256]{2,1,0:T(8,128)(2,1)S(1)}, u32[]{:S(2)}, u32[]{:S(2)}) %collective-permute-start.14) | collective-permute-done | bytes 131104 | tf_op jit(solution)/shard_map/ppermute | solution.py:303
  (67 shorter events, 22.7 us)
Async XLA Ops:
  6.5 82.3 %copy-start.10 = (bf16[4096,1,128]{2,0,1:T(8,128)(2,1)S(1)}, bf16[4096,1,128]{2,0,1:T(8,128)(2,1)}, u32[]{:S(2)}) copy-start(bf16[4096,1,128]{2,0,1:T(8,128)(2,1)} %param.9) | copy-start | bytes 3145732
  6.5 60.4 %all-gather.2.cloned.1.call-start = ((), (), s32[]{:S(2)}) async-start(), calls=%async_computation.3 | async-start | bytes 4718592 | tf_op jit(solution)/shard_map/all_gather | solution.py:318
  66.9 122.8 %collective-permute-start.12 = (bf16[8192,256]{1,0:T(8,128)(2,1)}, bf16[8192,256]{1,0:T(8,128)(2,1)}, u32[]{:S(2)}, u32[]{:S(2)}) collective-permute-start(bf16[8192,256]{1,0:T(8,128)(2,1)} %all-gather.2.cloned.1.call-done.refs_8_), channel_id=1, source_target_pairs={{0,1},{1,0},{2,3},{3,2},{4,5},{5,4},{6,7},{7,6},{8,9},{9,8},{10,11... | collective-permute-start | bytes 12582920 | tf_op jit(solution)/shard_map/ppermute | solution.py:307
  107.6 15.8 %all-to-all-start.1 = ((bf16[8,144,512]{2,1,0:T(8,128)(2,1)}), bf16[8,144,512]{2,1,0:T(8,128)(2,1)S(1)}, u32[]{:S(2)}, u32[]{:S(2)}) async-start(bf16[8,144,512]{2,1,0:T(8,128)(2,1)} %copy-done.2), calls=%async_computation.1 | async-start | bytes 2359296 | tf_op jit(solution)/shard_map/all_to_all | solution.py:329
  139.0 22.0 %collective-permute-start.6 = (bf16[32,8,128]{2,1,0:T(8,128)(2,1)S(1)}, bf16[32,8,128]{2,1,0:T(8,128)(2,1)S(1)}, u32[]{:S(2)}, u32[]{:S(2)}) collective-permute-start(bf16[32,8,128]{2,1,0:T(8,128)(2,1)S(1)} %bitcast.71), channel_id=1, source_target_pairs={{0,32},{1,33},{2,34},{3,35},{32,2},{33,3},{34,0},{35,1},{64,96},{6... | collective-permute-start | bytes 196616 | tf_op jit(solution)/shard_map/ppermute | solution.py:299
  158.1 5.8 %collective-permute-start.7 = (bf16[32,8,128]{2,1,0:T(8,128)(2,1)S(1)}, bf16[32,8,128]{2,1,0:T(8,128)(2,1)S(1)}, u32[]{:S(2)}, u32[]{:S(2)}) collective-permute-start(bf16[32,8,128]{2,1,0:T(8,128)(2,1)S(1)} %bitcast.72), channel_id=1, source_target_pairs={{0,2},{1,3},{2,0},{3,1},{32,34},{33,35},{34,32},{35,33},{64,66},{6... | collective-permute-start | bytes 196616 | tf_op jit(solution)/shard_map/ppermute | solution.py:299
  158.4 5.4 %collective-permute-start.8 = (bf16[32,8,128]{2,1,0:T(8,128)(2,1)S(1)}, bf16[32,8,128]{2,1,0:T(8,128)(2,1)S(1)}, u32[]{:S(2)}, u32[]{:S(2)}) collective-permute-start(bf16[32,8,128]{2,1,0:T(8,128)(2,1)S(1)} %bitcast.73), channel_id=1, source_target_pairs={{0,34},{1,35},{2,32},{3,33},{32,0},{33,1},{34,2},{35,3},{64,98},{6... | collective-permute-start | bytes 196616 | tf_op jit(solution)/shard_map/ppermute | solution.py:299
  163.9 15.2 %collective-permute-start.10 = (bf16[4,32,8,128]{3,2,1,0:T(8,128)(2,1)S(1)}, bf16[4,32,8,128]{3,2,1,0:T(8,128)(2,1)S(1)}, u32[]{:S(2)}, u32[]{:S(2)}) collective-permute-start(bf16[4,32,8,128]{3,2,1,0:T(8,128)(2,1)S(1)} %pad_maximum_fusion.1.refs_4_), channel_id=1, source_target_pairs={{0,128},{1,129},{2,130},{3,131},{32,160},{33,161},{34,162},{35,163... | collective-permute-start | bytes 786440 | tf_op jit(solution)/shard_map/ppermute | solution.py:299
  164.8 17.1 %collective-permute-start.11 = (bf16[4,32,8,128]{3,2,1,0:T(8,128)(2,1)S(1)}, bf16[4,32,8,128]{3,2,1,0:T(8,128)(2,1)S(1)}, u32[]{:S(2)}, u32[]{:S(2)}) collective-permute-start(bf16[4,32,8,128]{3,2,1,0:T(8,128)(2,1)S(1)} %pad_maximum_fusion.1.refs_4_), channel_id=1, source_target_pairs={{0,192},{1,193},{2,194},{3,195},{32,224},{33,225},{34,226},{35,227... | collective-permute-start | bytes 786440 | tf_op jit(solution)/shard_map/ppermute | solution.py:299
  166.8 7.2 %collective-permute-start = (bf16[32,8,128]{2,1,0:T(8,128)(2,1)S(1)}, bf16[32,8,128]{2,1,0:T(8,128)(2,1)S(1)}, u32[]{:S(2)}, u32[]{:S(2)}) collective-permute-start(bf16[32,8,128]{2,1,0:T(8,128)(2,1)S(1)} %bitcast.67), channel_id=1, source_target_pairs={{0,64},{1,65},{2,66},{3,67},{32,96},{33,97},{34,98},{35,99},{64,12... | collective-permute-start | bytes 196616 | tf_op jit(solution)/shard_map/ppermute | solution.py:299
  166.9 7.1 %collective-permute-start.1 = (bf16[32,8,128]{2,1,0:T(8,128)(2,1)S(1)}, bf16[32,8,128]{2,1,0:T(8,128)(2,1)S(1)}, u32[]{:S(2)}, u32[]{:S(2)}) collective-permute-start(bf16[32,8,128]{2,1,0:T(8,128)(2,1)S(1)} %bitcast.68), channel_id=1, source_target_pairs={{0,128},{1,129},{2,130},{3,131},{32,160},{33,161},{34,162},{35,163... | collective-permute-start | bytes 196616 | tf_op jit(solution)/shard_map/ppermute | solution.py:299
  174.0 4.3 %collective-permute-start.2 = (bf16[32,8,128]{2,1,0:T(8,128)(2,1)S(1)}, bf16[32,8,128]{2,1,0:T(8,128)(2,1)S(1)}, u32[]{:S(2)}, u32[]{:S(2)}) collective-permute-start(bf16[32,8,128]{2,1,0:T(8,128)(2,1)S(1)} %bitcast.69), channel_id=1, source_target_pairs={{0,192},{1,193},{2,194},{3,195},{32,224},{33,225},{34,226},{35,227... | collective-permute-start | bytes 196616 | tf_op jit(solution)/shard_map/ppermute | solution.py:299
  174.0 9.7 %collective-permute-start.9 = (bf16[4,32,8,128]{3,2,1,0:T(8,128)(2,1)S(1)}, bf16[4,32,8,128]{3,2,1,0:T(8,128)(2,1)S(1)}, u32[]{:S(2)}, u32[]{:S(2)}) collective-permute-start(bf16[4,32,8,128]{3,2,1,0:T(8,128)(2,1)S(1)} %pad_maximum_fusion.1.refs_4_), channel_id=1, source_target_pairs={{0,64},{1,65},{2,66},{3,67},{32,96},{33,97},{34,98},{35,99},{64,12... | collective-permute-start | bytes 786440 | tf_op jit(solution)/shard_map/ppermute | solution.py:299
  178.3 6.4 %collective-permute-start.3 = (bf16[4,32,8,128]{3,2,1,0:T(8,128)(2,1)S(1)}, bf16[4,32,8,128]{3,2,1,0:T(8,128)(2,1)S(1)}, u32[]{:S(2)}, u32[]{:S(2)}) collective-permute-start(bf16[4,32,8,128]{3,2,1,0:T(8,128)(2,1)S(1)} %pad_maximum_fusion.refs_0_), channel_id=1, source_target_pairs={{0,32},{1,33},{2,34},{3,35},{32,2},{33,3},{34,0},{35,1},{64,96},{6... | collective-permute-start | bytes 786440 | tf_op jit(solution)/shard_map/ppermute | solution.py:299
  179.1 8.0 %collective-permute-start.4 = (bf16[4,32,8,128]{3,2,1,0:T(8,128)(2,1)S(1)}, bf16[4,32,8,128]{3,2,1,0:T(8,128)(2,1)S(1)}, u32[]{:S(2)}, u32[]{:S(2)}) collective-permute-start(bf16[4,32,8,128]{3,2,1,0:T(8,128)(2,1)S(1)} %pad_maximum_fusion.refs_0_), channel_id=1, source_target_pairs={{0,2},{1,3},{2,0},{3,1},{32,34},{33,35},{34,32},{35,33},{64,66},{6... | collective-permute-start | bytes 786440 | tf_op jit(solution)/shard_map/ppermute | solution.py:299
  181.9 7.8 %collective-permute-start.5 = (bf16[4,32,8,128]{3,2,1,0:T(8,128)(2,1)S(1)}, bf16[4,32,8,128]{3,2,1,0:T(8,128)(2,1)S(1)}, u32[]{:S(2)}, u32[]{:S(2)}) collective-permute-start(bf16[4,32,8,128]{3,2,1,0:T(8,128)(2,1)S(1)} %pad_maximum_fusion.refs_0_), channel_id=1, source_target_pairs={{0,34},{1,35},{2,32},{3,33},{32,0},{33,1},{34,2},{35,3},{64,98},{6... | collective-permute-start | bytes 786440 | tf_op jit(solution)/shard_map/ppermute | solution.py:299
  196.5 1.3 collective-permute-start.13
  197.9 9.6 %collective-permute-start.20 = (bf16[2,128,256]{2,1,0:T(8,128)(2,1)S(1)}, bf16[2,128,256]{2,1,0:T(8,128)(2,1)S(1)}, u32[]{:S(2)}, u32[]{:S(2)}) collective-permute-start(bf16[2,128,256]{2,1,0:T(8,128)(2,1)S(1)} %pad_maximum_fusion.2), channel_id=1, source_target_pairs={{0,28},{4,0},{8,4},{12,8},{16,12},{20,16},{24,20},{28,24},{1,29},{... | collective-permute-start | bytes 393224 | tf_op jit(solution)/shard_map/ppermute | solution.py:303
  198.1 14.4 %collective-permute-start.19 = (bf16[2,128,256]{2,1,0:T(8,128)(2,1)S(1)}, bf16[2,128,256]{2,1,0:T(8,128)(2,1)S(1)}, u32[]{:S(2)}, u32[]{:S(2)}) collective-permute-start(bf16[2,128,256]{2,1,0:T(8,128)(2,1)S(1)} %pad_maximum_fusion.2), channel_id=1, source_target_pairs={{0,24},{4,28},{8,0},{12,4},{16,8},{20,12},{24,16},{28,20},{1,25},{... | collective-permute-start | bytes 393224 | tf_op jit(solution)/shard_map/ppermute | solution.py:303
  199.0 19.3 %collective-permute-start.18 = (bf16[2,128,256]{2,1,0:T(8,128)(2,1)S(1)}, bf16[2,128,256]{2,1,0:T(8,128)(2,1)S(1)}, u32[]{:S(2)}, u32[]{:S(2)}) collective-permute-start(bf16[2,128,256]{2,1,0:T(8,128)(2,1)S(1)} %pad_maximum_fusion.2), channel_id=1, source_target_pairs={{0,20},{4,24},{8,28},{12,0},{16,4},{20,8},{24,12},{28,16},{1,21},{... | collective-permute-start | bytes 393224 | tf_op jit(solution)/shard_map/ppermute | solution.py:303
  202.9 15.5 %collective-permute-start.17 = (bf16[2,128,256]{2,1,0:T(8,128)(2,1)S(1)}, bf16[2,128,256]{2,1,0:T(8,128)(2,1)S(1)}, u32[]{:S(2)}, u32[]{:S(2)}) collective-permute-start(bf16[2,128,256]{2,1,0:T(8,128)(2,1)S(1)} %pad_maximum_fusion.2), channel_id=1, source_target_pairs={{0,16},{4,20},{8,24},{12,28},{16,0},{20,4},{24,8},{28,12},{1,17},{... | collective-permute-start | bytes 393224 | tf_op jit(solution)/shard_map/ppermute | solution.py:303
  204.9 19.6 %collective-permute-start.16 = (bf16[2,128,256]{2,1,0:T(8,128)(2,1)S(1)}, bf16[2,128,256]{2,1,0:T(8,128)(2,1)S(1)}, u32[]{:S(2)}, u32[]{:S(2)}) collective-permute-start(bf16[2,128,256]{2,1,0:T(8,128)(2,1)S(1)} %pad_maximum_fusion.2), channel_id=1, source_target_pairs={{0,12},{4,16},{8,20},{12,24},{16,28},{20,0},{24,4},{28,8},{1,13},{... | collective-permute-start | bytes 393224 | tf_op jit(solution)/shard_map/ppermute | solution.py:303
  207.4 17.1 %collective-permute-start.15 = (bf16[2,128,256]{2,1,0:T(8,128)(2,1)S(1)}, bf16[2,128,256]{2,1,0:T(8,128)(2,1)S(1)}, u32[]{:S(2)}, u32[]{:S(2)}) collective-permute-start(bf16[2,128,256]{2,1,0:T(8,128)(2,1)S(1)} %pad_maximum_fusion.2), channel_id=1, source_target_pairs={{0,8},{4,12},{8,16},{12,20},{16,24},{20,28},{24,0},{28,4},{1,9},{5... | collective-permute-start | bytes 393224 | tf_op jit(solution)/shard_map/ppermute | solution.py:303
  212.5 15.9 %collective-permute-start.14 = (bf16[2,128,256]{2,1,0:T(8,128)(2,1)S(1)}, bf16[2,128,256]{2,1,0:T(8,128)(2,1)S(1)}, u32[]{:S(2)}, u32[]{:S(2)}) collective-permute-start(bf16[2,128,256]{2,1,0:T(8,128)(2,1)S(1)} %pad_maximum_fusion.2), channel_id=1, source_target_pairs={{0,4},{4,8},{8,12},{12,16},{16,20},{20,24},{24,28},{28,0},{1,5},{5... | collective-permute-start | bytes 393224 | tf_op jit(solution)/shard_map/ppermute | solution.py:303
  (10 other events, 102.5 us)
Sparse Core Ops, SparseCore 0:
  9.1 57.7 all-gather.1
